TPU v7x, 256 devices: a whole 4x4x8 slice. The times are simulated.
256 devices in a mesh: outer: 64 (over x, y_hi, z), inner: 4 (over y_lo, core).
Axes of the slice: x: 4, y: 4 (y_hi: 2, y_lo: 2; y = y_hi * 2 + y_lo), z: 8, core: 2. Of those that a mesh axis runs over, the one named last changes fastest.
Arguments:
- query_rows: bfloat16 [65536, 1024], P(('outer', 'inner')), may hold values from -8 to 8
- key_rows: bfloat16 [65536, 128], P(('outer', 'inner')), may hold values from -4 to 4
- value_rows: bfloat16 [65536, 128], P(('outer', 'inner')), may hold values from -6 to 6
- out_grad: bfloat16 [65536, 1024], P(('outer', 'inner')), may hold values from -6 to 6
- piece_ids: int32 [512], replicated, may hold values from 0 to 511, as said below
- key_pieces: int32 [512, 16], P('outer'), may hold values from -1 to 511, as said below
Outputs:
- query_grad: bfloat16 [65536, 1024], P(('outer', 'inner'))
- key_grad: bfloat16 [65536, 128], P(('outer', 'inner'))
- value_grad: bfloat16 [65536, 128], P(('outer', 'inner'))
Inputs may be any that keep to these rules, and one draw needn't show every extreme that they name: `piece_ids`: each piece once. Piece p is the one of tokens p * 128 to (p + 1) * 128 - 1 of the sequence. The slots g * 2 * 4 to (g + 1) * 2 * 4 - 1 hold, in some order, the pieces g * 4 to (g + 1) * 4 - 1 and (127 - g) * 4 to (128 - g) * 4 - 1. `key_pieces`: -1 marks an empty entry, in any position. Row s names its own piece piece_ids[s], no piece twice, only pieces no later than its own, and only pieces held by slots of the same group as s or of the group below it (group 0 with group 64 - 1), the group of slot s being s // 8.
All inputs are finite; a program needn't handle non-finite values.
Results may differ from a plain program's by a relative error of at most 0.04.
Values may be sent and summed in bfloat16 or wider, within the bound.
A program may use at most 64 MiB of HBM per device.

v0:
```python
import jax
import jax.numpy as jnp
from jax import lax
from jax.sharding import PartitionSpec as P

NEG_FILL = -1e30


def shifted(x, axis, by):
    count = lax.axis_size(axis)
    return lax.ppermute(x, axis, [(i, (i + by) % count) for i in range(count)])


def score_block(query_heads, key_set, scaling):
    return (
        jnp.einsum("qhd,kd->hqk", query_heads, key_set, preferred_element_type=jnp.float32)
        * scaling
    )


def token_mask(query_set, listing, key_pair, row_count):
    piece_rows = row_count // 2
    listed = jnp.any(listing[:, None, :] == key_pair[None, :, None], axis=2)
    same_piece = query_set[:, None] == key_pair[None, :]
    listed_rows = jnp.repeat(jnp.repeat(listed, piece_rows, axis=0), piece_rows, axis=1)
    same_rows = jnp.repeat(jnp.repeat(same_piece, piece_rows, axis=0), piece_rows, axis=1)
    offsets = jnp.arange(row_count) % piece_rows
    causal = offsets[None, :] <= offsets[:, None]
    return listed_rows & (jnp.logical_not(same_rows) | causal)


def back_block(query_heads, grad_heads, log_norm, row_delta, key_set, value_set, allowed, scaling):
    scores = score_block(query_heads, key_set, scaling)
    weights = jnp.where(allowed[None], jnp.exp(scores - log_norm[:, :, None]), 0.0)
    weights_low = weights.astype(jnp.bfloat16)
    dweights = jnp.einsum("qhd,kd->hqk", grad_heads, value_set, preferred_element_type=jnp.float32)
    dscores = (weights * (dweights - row_delta[:, :, None])).astype(jnp.bfloat16)
    query_term = (
        jnp.einsum("hqk,kd->qhd", dscores, key_set, preferred_element_type=jnp.float32) * scaling
    )
    key_term = (
        jnp.einsum("hqk,qhd->kd", dscores, query_heads, preferred_element_type=jnp.float32)
        * scaling
    )
    value_term = jnp.einsum(
        "hqk,qhd->kd", weights_low, grad_heads, preferred_element_type=jnp.float32
    )
    return (query_term, jnp.stack([key_term, value_term]))


def per_device(query_rows, key_rows, value_rows, out_grad, piece_ids, key_pieces):
    row_count = query_rows.shape[0]
    head_width = key_rows.shape[1]
    head_count = query_rows.shape[1] // head_width
    scaling = head_width ** (-0.5)
    inner_count = lax.axis_size("inner")
    outer_count = lax.axis_size("outer")
    outer_idx = lax.axis_index("outer")
    inner_idx = lax.axis_index("inner")
    group_slots = 2 * inner_count
    listed_width = key_pieces.shape[1]
    own_ids = lax.dynamic_slice_in_dim(piece_ids, outer_idx * group_slots, group_slots, 0)
    lower_group = (outer_idx + outer_count - 1) % outer_count
    lower_ids = lax.dynamic_slice_in_dim(piece_ids, lower_group * group_slots, group_slots, 0)
    own_pairs = own_ids.reshape(inner_count, 2)
    lower_pairs = lower_ids.reshape(inner_count, 2)
    group_lists = key_pieces.reshape(inner_count, 2, listed_width)
    my_pieces = lax.dynamic_index_in_dim(own_pairs, inner_idx, 0, keepdims=False)
    my_lists = lax.dynamic_index_in_dim(group_lists, inner_idx, 0, keepdims=False)
    set_pieces = jnp.stack([own_pairs, lower_pairs], axis=1).reshape(2 * inner_count, 2)
    set_masks = jax.vmap(lambda key_pair: token_mask(my_pieces, my_lists, key_pair, row_count))(
        set_pieces
    )
    local_kv = jnp.stack([key_rows, value_rows])
    lower_kv = shifted(local_kv, "outer", 1)
    both_sets = jnp.stack([local_kv, lower_kv])
    gathered = lax.all_gather(both_sets[None], "inner", axis=0, tiled=True).reshape(
        2 * inner_count, 2, row_count, head_width
    )
    key_sets = gathered[:, 0]
    value_sets = gathered[:, 1]
    query_heads = query_rows.reshape(row_count, head_count, head_width)
    grad_heads = out_grad.reshape(row_count, head_count, head_width)

    def stat_step(carried, inputs):
        key_set, allowed = inputs
        scores = score_block(query_heads, key_set, scaling)
        running_max = jnp.maximum(
            carried[0], jnp.max(jnp.where(allowed[None], scores, NEG_FILL), axis=2)
        )
        running_sum = carried[1] * jnp.exp(carried[0] - running_max) + jnp.sum(
            jnp.where(allowed[None], jnp.exp(scores - running_max[:, :, None]), 0.0), axis=2
        )
        return ((running_max, running_sum), None)

    initial = (
        jnp.full((head_count, row_count), NEG_FILL, jnp.float32),
        jnp.zeros((head_count, row_count), jnp.float32),
    )
    (running_max, running_sum), _ = lax.scan(stat_step, initial, (key_sets, set_masks))
    log_norm = running_max + jnp.log(running_sum)

    def output_step(carried, inputs):
        key_set, value_set, allowed = inputs
        scores = score_block(query_heads, key_set, scaling)
        weights_low = jnp.where(allowed[None], jnp.exp(scores - log_norm[:, :, None]), 0.0).astype(
            jnp.bfloat16
        )
        return (
            carried
            + jnp.einsum("hqk,kd->qhd", weights_low, value_set, preferred_element_type=jnp.float32),
            None,
        )

    output_sum, _ = lax.scan(
        output_step,
        jnp.zeros((row_count, head_count, head_width), jnp.float32),
        (key_sets, value_sets, set_masks),
    )
    attended = output_sum.astype(jnp.bfloat16)
    row_delta = jnp.sum(grad_heads.astype(jnp.float32) * attended.astype(jnp.float32), axis=2).T

    def back_step(carried, inputs):
        key_set, value_set, allowed = inputs
        query_term, kv_term = back_block(
            query_heads, grad_heads, log_norm, row_delta, key_set, value_set, allowed, scaling
        )
        return (carried + query_term, kv_term)

    query_sum, kv_terms = lax.scan(
        back_step,
        jnp.zeros((row_count, head_count, head_width), jnp.float32),
        (key_sets, value_sets, set_masks),
    )
    kv_terms = kv_terms.reshape(inner_count, 2, 2, row_count, head_width)
    summed = lax.psum_scatter(kv_terms, "inner", scatter_dimension=0, tiled=True)
    own_part = summed[0, 0]
    lower_part = summed[0, 1]
    returned = shifted(lower_part, "outer", -1)
    kv_total = own_part + returned
    query_grad = query_sum.reshape(row_count, head_count * head_width).astype(jnp.bfloat16)
    return (query_grad, kv_total[0].astype(jnp.bfloat16), kv_total[1].astype(jnp.bfloat16))


def solution(mesh):
    return jax.shard_map(
        per_device,
        mesh=mesh,
        in_specs=(
            P(("outer", "inner"), None),
            P(("outer", "inner"), None),
            P(("outer", "inner"), None),
            P(("outer", "inner"), None),
            P(),
            P("outer", None),
        ),
        out_specs=(
            P(("outer", "inner"), None),
            P(("outer", "inner"), None),
            P(("outer", "inner"), None),
        ),
        check_vma=False,
    )
```

profile of v0, /device:TPU:1, one launch (start us, length us, event | category | flops | bytes accessed | tf_op | source)
XLA Modules:
  0.0 183.7 jit_solution(8132957249685882394)
XLA Ops:
  7.2 0.9 fusion.51
  8.2 2.5 %collective-permute-start = (bf16[2,256,128]{2,1,0:T(8,128)(2,1)S(1)}, bf16[2,256,128]{2,1,0:T(8,128)(2,1)S(1)}, u32[]{:S(2)}, u32[]{:S(2)}) collective-permute-start(bf16[2,256,128]{2,1,0:T(8,128)(2,1)S(1)} %get-tuple-element.315), channel_id=1, source_target_pairs={{0,4},{4,8},{8,12},{12,16},{16,20},{20,24},{24,28},{28,32},{32,36}... | collective-permute-start | bytes 393224 | tf_op jit(solution)/shard_map/ppermute | solution.py:11
  10.7 12.0 %collective-permute-done = bf16[2,256,128]{2,1,0:T(8,128)(2,1)S(1)} collective-permute-done((bf16[2,256,128]{2,1,0:T(8,128)(2,1)S(1)}, bf16[2,256,128]{2,1,0:T(8,128)(2,1)S(1)}, u32[]{:S(2)}, u32[]{:S(2)}) %collective-permute-start) | collective-permute-done | bytes 131104 | tf_op jit(solution)/shard_map/ppermute | solution.py:11
  22.7 0.7 pad_maximum_fusion
  23.5 0.8 fusion.52
  25.5 1.2 copy.46
  28.0 15.1 %all-gather.3.cloned.1.call-done = bf16[8,2,256,128]{3,2,0,1:T(8,128)(2,1)} async-done(((bf16[2,2,256,128]{3,2,0,1:T(8,128)(2,1)}), bf16[8,2,256,128]{3,2,0,1:T(8,128)(2,1)}) %all-gather.3.cloned.1.call-update) | async-done | bytes 1048592 | tf_op jit(solution)/shard_map/all_gather | solution.py:77
  43.1 2.3 %slice_bitcast_fusion = (bf16[8,256,128]{2,1,0:T(8,128)(2,1)}, bf16[8,256,128]{2,1,0:T(8,128)(2,1)}) fusion(bf16[8,2,256,128]{3,2,0,1:T(8,128)(2,1)} %all-gather.3.cloned.1.call-done), kind=kLoop, calls=%fused_computation.62 | loop fusion | bytes 2097152 | tf_op jit(solution)/shard_map/squeeze | solution.py:81
  45.4 14.8 %while.37 = (s32[]{:T(128)}, f32[8,256]{1,0:T(8,128)S(1)}, f32[8,256]{1,0:T(8,128)S(1)}, pred[8,256,256]{1,2,0:T(8,128)(4,1)S(1)}, bf16[8,256,128]{2,1,0:T(8,128...) while((s32[]{:T(128)}, f32[8,256]{1,0:T(8,128)S(1)}, f32[8,256]{1,0:T(8,128)S(1)}, ...), condition=%wide.region_4.5_spmd.clone, body=%wide.region_1.4_spmd.clone.sunk | while | flops 137897984 | bytes 5152880 | solution.py:100
  45.4 1.3 fusion.85
  47.3 1.3 fusion.85
  49.1 1.3 fusion.85
  51.0 1.3 fusion.85
  52.8 1.3 fusion.85
  54.7 1.3 fusion.85
  56.5 1.3 fusion.85
  58.4 1.3 fusion.85
  60.2 23.9 %while.38 = (s32[]{:T(128)}, f32[256,8,128]{0,2,1:T(8,128)}, bf16[8,256,128]{2,1,0:T(8,128)(2,1)}, pred[8,256,256]{1,2,0:T(8,128)(4,1)S(1)}, bf16[8,256,128]{2,1...) while((s32[]{:T(128)}, f32[256,8,128]{0,2,1:T(8,128)}, ...), condition=%wide.region_6.7_spmd.clone, body=%wide.region_5.6_spmd.clone.sunk | while | flops 271056896 | bytes 2958962 | solution.py:115
  60.3 2.6 %fusion.91 = f32[256,8,128]{0,2,1:T(8,128)} fusion(bf16[256,8,128]{2,0,1:T(8,128)(2,1)S(1)} %get-tuple-element.510, f32[256,8,128]{0,2,1:T(8,128)} %get-tuple-element.497, f32[8,256]{1,0:T(8,128)S(1)} %get-tuple-element.511, pred[256,256]{0,1:T(8,128)(4,1)S(1)} %dynamic-slice_bitcast_fusion.9, pred[]{:T(512)S(6)} %compare.13, ...), kind=kOutput, calls=%fused_computation.20.clone.1 | convolution fusion | flops 271056896 | bytes 2827776 | tf_op jit(solution)/shard_map/while/body/eval_jaxpr/hqk,kd->qhd/dot_general | solution.py:111
  62.9 3.0 %fusion.91 = f32[256,8,128]{0,2,1:T(8,128)} fusion(bf16[256,8,128]{2,0,1:T(8,128)(2,1)S(1)} %get-tuple-element.510, f32[256,8,128]{0,2,1:T(8,128)} %get-tuple-element.497, f32[8,256]{1,0:T(8,128)S(1)} %get-tuple-element.511, pred[256,256]{0,1:T(8,128)(4,1)S(1)} %dynamic-slice_bitcast_fusion.9, pred[]{:T(512)S(6)} %compare.13, ...), kind=kOutput, calls=%fused_computation.20.clone.1 | convolution fusion | flops 271056896 | bytes 2827776 | tf_op jit(solution)/shard_map/while/body/eval_jaxpr/hqk,kd->qhd/dot_general | solution.py:111
  65.9 3.0 %fusion.91 = f32[256,8,128]{0,2,1:T(8,128)} fusion(bf16[256,8,128]{2,0,1:T(8,128)(2,1)S(1)} %get-tuple-element.510, f32[256,8,128]{0,2,1:T(8,128)} %get-tuple-element.497, f32[8,256]{1,0:T(8,128)S(1)} %get-tuple-element.511, pred[256,256]{0,1:T(8,128)(4,1)S(1)} %dynamic-slice_bitcast_fusion.9, pred[]{:T(512)S(6)} %compare.13, ...), kind=kOutput, calls=%fused_computation.20.clone.1 | convolution fusion | flops 271056896 | bytes 2827776 | tf_op jit(solution)/shard_map/while/body/eval_jaxpr/hqk,kd->qhd/dot_general | solution.py:111
  69.0 3.0 %fusion.91 = f32[256,8,128]{0,2,1:T(8,128)} fusion(bf16[256,8,128]{2,0,1:T(8,128)(2,1)S(1)} %get-tuple-element.510, f32[256,8,128]{0,2,1:T(8,128)} %get-tuple-element.497, f32[8,256]{1,0:T(8,128)S(1)} %get-tuple-element.511, pred[256,256]{0,1:T(8,128)(4,1)S(1)} %dynamic-slice_bitcast_fusion.9, pred[]{:T(512)S(6)} %compare.13, ...), kind=kOutput, calls=%fused_computation.20.clone.1 | convolution fusion | flops 271056896 | bytes 2827776 | tf_op jit(solution)/shard_map/while/body/eval_jaxpr/hqk,kd->qhd/dot_general | solution.py:111
  72.0 3.0 %fusion.91 = f32[256,8,128]{0,2,1:T(8,128)} fusion(bf16[256,8,128]{2,0,1:T(8,128)(2,1)S(1)} %get-tuple-element.510, f32[256,8,128]{0,2,1:T(8,128)} %get-tuple-element.497, f32[8,256]{1,0:T(8,128)S(1)} %get-tuple-element.511, pred[256,256]{0,1:T(8,128)(4,1)S(1)} %dynamic-slice_bitcast_fusion.9, pred[]{:T(512)S(6)} %compare.13, ...), kind=kOutput, calls=%fused_computation.20.clone.1 | convolution fusion | flops 271056896 | bytes 2827776 | tf_op jit(solution)/shard_map/while/body/eval_jaxpr/hqk,kd->qhd/dot_general | solution.py:111
  75.0 3.0 %fusion.91 = f32[256,8,128]{0,2,1:T(8,128)} fusion(bf16[256,8,128]{2,0,1:T(8,128)(2,1)S(1)} %get-tuple-element.510, f32[256,8,128]{0,2,1:T(8,128)} %get-tuple-element.497, f32[8,256]{1,0:T(8,128)S(1)} %get-tuple-element.511, pred[256,256]{0,1:T(8,128)(4,1)S(1)} %dynamic-slice_bitcast_fusion.9, pred[]{:T(512)S(6)} %compare.13, ...), kind=kOutput, calls=%fused_computation.20.clone.1 | convolution fusion | flops 271056896 | bytes 2827776 | tf_op jit(solution)/shard_map/while/body/eval_jaxpr/hqk,kd->qhd/dot_general | solution.py:111
  78.1 3.0 %fusion.91 = f32[256,8,128]{0,2,1:T(8,128)} fusion(bf16[256,8,128]{2,0,1:T(8,128)(2,1)S(1)} %get-tuple-element.510, f32[256,8,128]{0,2,1:T(8,128)} %get-tuple-element.497, f32[8,256]{1,0:T(8,128)S(1)} %get-tuple-element.511, pred[256,256]{0,1:T(8,128)(4,1)S(1)} %dynamic-slice_bitcast_fusion.9, pred[]{:T(512)S(6)} %compare.13, ...), kind=kOutput, calls=%fused_computation.20.clone.1 | convolution fusion | flops 271056896 | bytes 2827776 | tf_op jit(solution)/shard_map/while/body/eval_jaxpr/hqk,kd->qhd/dot_general | solution.py:111
  81.1 3.0 %fusion.91 = f32[256,8,128]{0,2,1:T(8,128)} fusion(bf16[256,8,128]{2,0,1:T(8,128)(2,1)S(1)} %get-tuple-element.510, f32[256,8,128]{0,2,1:T(8,128)} %get-tuple-element.497, f32[8,256]{1,0:T(8,128)S(1)} %get-tuple-element.511, pred[256,256]{0,1:T(8,128)(4,1)S(1)} %dynamic-slice_bitcast_fusion.9, pred[]{:T(512)S(6)} %compare.13, ...), kind=kOutput, calls=%fused_computation.20.clone.1 | convolution fusion | flops 271056896 | bytes 2827776 | tf_op jit(solution)/shard_map/while/body/eval_jaxpr/hqk,kd->qhd/dot_general | solution.py:111
  84.1 1.4 multiply_reduce_fusion
  85.5 45.2 %while.39 = (s32[]{:T(128)}, f32[256,8,128]{0,2,1:T(8,128)S(1)}, f32[8,2,256,128]{3,2,1,0:T(8,128)}, bf16[8,256,128]{2,1,0:T(8,128)(2,1)}, pred[8,256,256]{1,2,0...) while((s32[]{:T(128)}, f32[256,8,128]{0,2,1:T(8,128)S(1)}, ...), condition=%wide.region_9.10_spmd.clone, body=%wide.region_8.9_spmd.clone.sunk | while | flops 675643392 | bytes 14827675 | solution.py:130
  85.5 1.4 fusion.102
  87.4 1.3 fusion.103
  89.1 1.3 fusion.104
  91.2 1.4 fusion.102
  93.0 1.3 fusion.103
  94.8 1.3 fusion.104
  96.1 0.7 fusion.106
  96.8 1.4 fusion.102
  98.7 1.3 fusion.103
  100.4 1.3 fusion.104
  101.7 0.7 fusion.106
  102.4 1.4 fusion.102
  104.3 1.3 fusion.103
  106.0 1.3 fusion.104
  107.4 0.7 fusion.106
  108.1 1.4 fusion.102
  110.0 1.3 fusion.103
  111.7 1.3 fusion.104
  113.0 0.7 fusion.106
  113.7 1.4 fusion.102
  115.6 1.3 fusion.103
  117.3 1.3 fusion.104
  118.6 0.7 fusion.106
  119.4 1.4 fusion.102
  121.2 1.3 fusion.103
  123.0 1.3 fusion.104
  124.3 0.7 fusion.106
  125.0 1.4 fusion.102
  126.9 1.3 fusion.103
  128.6 1.3 fusion.104
  129.9 0.7 fusion.106
  130.7 31.8 %reduce-scatter.2.cloned.1.call-done = f32[1,2,2,256,128]{4,3,2,1,0:T(8,128)} async-done(((f32[4,2,2,256,128]{4,3,2,1,0:T(8,128)}), f32[1,2,2,256,128]{4,3,2,1,0:T(8,128)}) %reduce-scatter.2.cloned.1.call-update) | async-done | bytes 524304 | tf_op jit(solution)/shard_map/reduce_scatter | solution.py:136
  162.5 1.0 slice_bitcast_fusion.2
  163.5 7.4 %collective-permute-start.1 = (f32[2,256,128]{2,1,0:T(8,128)S(1)}, f32[2,256,128]{2,1,0:T(8,128)S(1)}, u32[]{:S(2)}, u32[]{:S(2)}) collective-permute-start(f32[2,256,128]{2,1,0:T(8,128)S(1)} %slice_bitcast_fusion.2), channel_id=1, source_target_pairs={{0,252},{4,0},{8,4},{12,8},{16,12},{20,16},{24,20},{28,24},{32,28}... | collective-permute-start | bytes 786440 | tf_op jit(solution)/shard_map/ppermute | solution.py:11
  171.0 1.0 copy.55
  172.0 4.2 %collective-permute-done.1 = f32[2,256,128]{2,1,0:T(8,128)S(1)} collective-permute-done((f32[2,256,128]{2,1,0:T(8,128)S(1)}, f32[2,256,128]{2,1,0:T(8,128)S(1)}, u32[]{:S(2)}, u32[]{:S(2)}) %collective-permute-start.1) | collective-permute-done | bytes 262176 | tf_op jit(solution)/shard_map/ppermute | solution.py:11
  (115 shorter events, 14.7 us)
Async XLA Ops:
  7.2 17.7 %copy-start = (s32[8,16]{1,0:T(8,128)S(1)}, s32[8,16]{1,0:T(8,128)}, u32[]{:S(2)}) copy-start(s32[8,16]{1,0:T(8,128)} %param.17) | copy-start | bytes 1540
  7.2 19.9 %copy-start.1 = (bf16[256,1024]{1,0:T(8,128)(2,1)S(1)}, bf16[256,1024]{1,0:T(8,128)(2,1)}, u32[]{:S(2)}) copy-start(bf16[256,1024]{1,0:T(8,128)(2,1)} %param.12) | copy-start | bytes 1572868
  7.2 35.9 %all-gather.3.cloned.1.call-start = ((), (), s32[]{:S(2)}) async-start(), calls=%async_computation.2 | async-start | bytes 1310720 | tf_op jit(solution)/shard_map/all_gather | solution.py:77
  8.2 14.5 %collective-permute-start = (bf16[2,256,128]{2,1,0:T(8,128)(2,1)S(1)}, bf16[2,256,128]{2,1,0:T(8,128)(2,1)S(1)}, u32[]{:S(2)}, u32[]{:S(2)}) collective-permute-start(bf16[2,256,128]{2,1,0:T(8,128)(2,1)S(1)} %get-tuple-element.315), channel_id=1, source_target_pairs={{0,4},{4,8},{8,12},{12,16},{16,20},{20,24},{24,28},{28,32},{32,36}... | collective-permute-start | bytes 393224 | tf_op jit(solution)/shard_map/ppermute | solution.py:11
  23.5 139.0 %reduce-scatter.2.cloned.1.call-start = ((), (), s32[]{:S(2)}) async-start(), calls=%async_computation.1 | async-start | bytes 2621440 | tf_op jit(solution)/shard_map/reduce_scatter | solution.py:136
  162.5 13.7 %copy-start.2 = (f32[1,2,2,256,128]{4,3,2,1,0:T(8,128)S(1)}, f32[1,2,2,256,128]{4,3,2,1,0:T(8,128)}, u32[]{:S(2)}) copy-start(f32[1,2,2,256,128]{4,3,2,1,0:T(8,128)} %reduce-scatter.2.cloned.1.call-done) | copy-start | bytes 1572868
  163.5 12.7 %collective-permute-start.1 = (f32[2,256,128]{2,1,0:T(8,128)S(1)}, f32[2,256,128]{2,1,0:T(8,128)S(1)}, u32[]{:S(2)}, u32[]{:S(2)}) collective-permute-start(f32[2,256,128]{2,1,0:T(8,128)S(1)} %slice_bitcast_fusion.2), channel_id=1, source_target_pairs={{0,252},{4,0},{8,4},{12,8},{16,12},{20,16},{24,20},{28,24},{32,28}... | collective-permute-start | bytes 786440 | tf_op jit(solution)/shard_map/ppermute | solution.py:11
Sparse Core Ops, SparseCore 0:
  23.6 19.5 all-gather.2
  130.8 31.6 reduce-scatter.1
where the time goes:
time: 186 us; the launch traced here: 184 us
  matrix products  73.3 us (39%)
  waiting for transfers between devices  63.2 us (34%)
  between operations  14.2 us (8%)
  other arithmetic  13.3 us (7%)
  starting transfers between devices  10 us (5%)
  local copies, waits for them, and re-layouts  8.87 us (5%)
    reduce_scatter x1, waiting for transfers between devices, per_device(): lax.psum_scatter(kv_terms, 'inner', scatter_dimension=0, tiled=True)  31.8 us
    dot_general x8, matrix products, output_step(): jnp.einsum('hqk,kd->qhd', weights_low, value_set, preferred_element_type=...  23.8 us
    dot_general x16, matrix products, score_block(): jnp.einsum('qhd,kd->hqk', query_heads, key_set, preferred_element_type=jn...  21.9 us
    ppermute x2, waiting for transfers between devices, shifted(): return lax.ppermute(x, axis, [(i, (i + by) % count) for i in range(count)])  16.2 us
    all_gather x1, waiting for transfers between devices, per_device(): lax.all_gather(both_sets[None], 'inner', axis=0, tiled=True)  15.1 us
    dot_general x8, matrix products, back_block(): jnp.einsum('hqk,kd->qhd', dscores, key_set, preferred_element_type=jnp.fl...  10.5 us
    dot_general x8, matrix products, back_block(): jnp.einsum('qhd,kd->hqk', grad_heads, value_set, preferred_element_type=j...  10.3 us
    ppermute x2, starting transfers between devices, shifted(): return lax.ppermute(x, axis, [(i, (i + by) % count) for i in range(count)])  9.94 us
  transfers between devices with their start and end apart: 4, of which 4 were waited for; matrix products, arithmetic and copies ran while one was open for 3% of the time, Pallas kernels for 0%

commit v1 on v0

v1 whole, which is shorter than its diff:
```python
import functools

import jax
import jax.numpy as jnp
from jax import lax
from jax.experimental import pallas as pl
from jax.experimental.pallas import tpu as pltpu
from jax.sharding import PartitionSpec as P

MESH = pl.DeviceIdType.MESH
F32 = jnp.float32
BF16 = jnp.bfloat16
LOG2E = 1.4426950408889634
FILL = -1e30


def dot_nt(a, b):
    return lax.dot_general(a, b, (((1,), (1,)), ((), ())), preferred_element_type=F32)


def dot_nn(a, b):
    return lax.dot_general(a, b, (((1,), (0,)), ((), ())), preferred_element_type=F32)


def kernel(
    outer_count,
    heads,
    q_ref,
    g_ref,
    k_ref,
    v_ref,
    ids_hbm,
    lists_hbm,
    dq_ref,
    dk_ref,
    dv_ref,
    kv,
    qg,
    qgt,
    kt,
    prob,
    dprob,
    top,
    total,
    dtotal,
    bias,
    stat,
    factor,
    delta,
    term,
    term_in,
    own_term,
    dq_out,
    dq_in,
    ids_ref,
    lists_ref,
    load_sem,
    kv_send,
    kv_recv,
    qg_send,
    qg_recv,
    stat_sem,
    term_send,
    term_recv,
    dq_sem,
):
    rows = k_ref.shape[0]
    width = k_ref.shape[1]
    piece = rows // 2
    tiles = 2 * heads
    half = heads * rows
    scale = width**-0.5
    scale2 = scale * LOG2E

    outer = lax.axis_index("outer")
    inner = lax.axis_index("inner")
    core = lax.rem(inner, 2)
    other = inner + 1 - 2 * core
    across = lax.rem(inner + 2, 4)
    up = lax.rem(outer + 1, outer_count)
    down = lax.rem(outer + outer_count - 1, outer_count)
    sibling = (outer, other)
    beside = (outer, across)

    def remote(src, dst, send, recv, device):
        return pltpu.make_async_remote_copy(
            src_ref=src, dst_ref=dst, send_sem=send, recv_sem=recv, device_id=device, device_id_type=MESH
        )

    loads_ids = [
        pltpu.make_async_copy(ids_hbm, ids_ref, load_sem.at[4]),
        pltpu.make_async_copy(lists_hbm, lists_ref, load_sem.at[5]),
    ]
    for c in loads_ids:
        c.start()
    loads_kv = [
        pltpu.make_async_copy(k_ref, kv.at[0, 0], load_sem.at[0]),
        pltpu.make_async_copy(v_ref, kv.at[1, 0], load_sem.at[1]),
    ]
    for c in loads_kv:
        c.start()
    loads_q = []
    for which, src in ((0, q_ref), (1, g_ref)):
        for h in range(heads):
            loads_q.append(
                pltpu.make_async_copy(
                    src.at[:, pl.ds(h * width, width)],
                    qg.at[which, pl.ds(h * rows, rows)],
                    load_sem.at[2 + which],
                )
            )
    for c in loads_q:
        c.start()

    barrier = pltpu.get_barrier_semaphore()
    for device in (sibling, beside, (up, inner), (down, inner), (up, across), (down, across)):
        pl.semaphore_signal(barrier, inc=1, device_id=device, device_id_type=MESH)
    pl.semaphore_wait(barrier, 6)

    kv_sends = []
    for slot, device in ((2, (up, inner)), (3, (up, across)), (1, beside)):
        for which, src in ((0, k_ref), (1, v_ref)):
            index = 2 * slot + which
            c = remote(src, kv.at[which, slot], kv_send.at[index], kv_recv.at[index], device)
            c.start()
            kv_sends.append((index, c))
    by_index = dict(kv_sends)
    for which, src in ((0, q_ref), (1, g_ref)):
        for h in range(heads):
            c = remote(
                src.at[:, pl.ds(h * width, width)],
                qg.at[which, pl.ds(half + h * rows, rows)],
                qg_send.at[which],
                qg_recv.at[which],
                sibling,
            )
            c.start()

    for c in loads_ids:
        c.wait()
    slot_index = lax.broadcasted_iota(jnp.int32, (8, 1), 0)
    ids = jnp.zeros((8, 1), jnp.int32)
    for slot, (group, device) in enumerate(
        ((outer, inner), (outer, across), (down, inner), (down, across))
    ):
        for a in range(2):
            ids = jnp.where(slot_index == 2 * slot + a, ids_ref[group * 8 + device * 2 + a], ids)
    for who, device in ((0, inner), (1, other)):
        parts = []
        for a in range(2):
            row = lists_ref[pl.ds(2 * device + a, 1), :]
            hit = jnp.max(jnp.where(row == ids, 1.0, 0.0), axis=1, keepdims=True)
            parts.append(jnp.broadcast_to((hit - 1.0) * (-FILL), (8, piece)))
        both = jnp.concatenate(parts, axis=1)
        for j in range(8):
            bias[who, j] = jnp.broadcast_to(both[j : j + 1], (8, rows))

    causal = lax.broadcasted_iota(jnp.int32, (piece, piece), 0) <= lax.broadcasted_iota(
        jnp.int32, (piece, piece), 1
    )

    def scores(slot, who):
        def head(h, _):
            t = who * heads + h
            lanes = pl.ds(pl.multiple_of(t * rows, rows), rows)
            s = dot_nt(kv[0, slot], qg[0, lanes, :])
            g = dot_nt(kv[1, slot], qg[1, lanes, :])
            for a in range(2):
                sa = s[a * piece : (a + 1) * piece]
                ga = g[a * piece : (a + 1) * piece]
                if slot == 0 and who == 0:
                    cut = jnp.where(causal, sa[:, a * piece : (a + 1) * piece], FILL)
                    sa = jnp.concatenate(
                        [cut, sa[:, piece:]] if a == 0 else [sa[:, :piece], cut], axis=1
                    )
                s3 = sa.reshape(piece // 8, 8, rows)
                g3 = ga.reshape(piece // 8, 8, rows)
                m = jnp.max(s3, axis=0)
                p = jnp.exp2((s3 - m[None]) * scale2)
                place = pl.ds(slot * rows + a * piece, piece)
                prob[place, lanes] = p.reshape(piece, rows).astype(BF16)
                dprob[place, lanes] = ga.astype(BF16)
                top[t, 2 * slot + a] = m * scale2
                total[t, 2 * slot + a] = jnp.sum(p, axis=0)
                dtotal[t, 2 * slot + a] = jnp.sum(p * g3, axis=0)
            return 0

        lax.fori_loop(0, heads, head, 0, unroll=True)

    def transposed(who):
        def head(h, _):
            lanes = pl.ds(pl.multiple_of((who * heads + h) * rows, rows), rows)
            qgt[0, :, lanes] = qg[0, lanes, :].T
            qgt[1, :, lanes] = qg[1, lanes, :].T
            return 0

        lax.fori_loop(0, heads, head, 0, unroll=True)

    def transposed_keys(slot):
        kt[:, pl.ds(slot * rows, rows)] = kv[0, slot].T

    for c in loads_kv:
        c.wait()
    for which in range(2):
        pltpu.make_async_copy(
            qg.at[which, pl.ds(half, half)], qg.at[which, pl.ds(0, half)], load_sem.at[2 + which]
        ).wait()
    scores(0, 0)
    transposed(0)
    transposed_keys(0)
    qg_all = [
        remote(
            qg.at[which, pl.ds(0, half)],
            qg.at[which, pl.ds(half, half)],
            qg_send.at[which],
            qg_recv.at[which],
            sibling,
        )
        for which in range(2)
    ]
    for c in qg_all:
        c.wait_recv()
    scores(0, 1)
    transposed(1)
    for slot in (1, 2, 3):
        for which in range(2):
            by_index[2 * slot + which].wait_recv()
        scores(slot, 0)
        scores(slot, 1)
        transposed_keys(slot)

    for who in range(2):

        def local(h, _, who=who):
            t = who * heads + h
            mj = top[t] + bias[who]
            m = jnp.max(jnp.max(mj, axis=0), axis=0, keepdims=True)
            w = jnp.exp2(mj - m[None])
            top[t] = w
            stat[0, 0, pl.ds(t, 1)] = m
            stat[0, 1, pl.ds(t, 1)] = jnp.sum(jnp.sum(w * total[t], axis=0), axis=0, keepdims=True)
            stat[0, 2, pl.ds(t, 1)] = jnp.sum(jnp.sum(w * dtotal[t], axis=0), axis=0, keepdims=True)
            return 0

        lax.fori_loop(0, heads, local, 0, unroll=True)
    stat_copy = remote(stat.at[0], stat.at[1], stat_sem.at[0], stat_sem.at[1], sibling)
    stat_copy.start()
    stat_copy.wait()
    mine = [stat[0, c] for c in range(3)]
    theirs = [jnp.concatenate([stat[1, c, heads:], stat[1, c, :heads]], axis=0) for c in range(3)]
    m = jnp.maximum(mine[0], theirs[0])
    e_mine = jnp.exp2(mine[0] - m)
    e_theirs = jnp.exp2(theirs[0] - m)
    inverse = 1.0 / (mine[1] * e_mine + theirs[1] * e_theirs)
    factor[...] = e_mine * inverse
    d = (mine[2] * e_mine + theirs[2] * e_theirs) * inverse
    for t in range(tiles):
        delta[:, pl.ds(t * rows, rows)] = jnp.broadcast_to(d[t : t + 1], (16, rows)).astype(BF16)

    def gradients(slot):
        def tile(t, _):
            lanes = pl.ds(pl.multiple_of(t * rows, rows), rows)
            f = factor[pl.ds(t, 1)]
            de = delta[:, lanes]
            for a in range(2):
                r = (top[t, 2 * slot + a] * f).astype(BF16)
                r = jnp.concatenate([r, r], axis=0)
                place = pl.ds(slot * rows + a * piece, piece)
                p = prob[place, lanes].reshape(piece // 16, 16, rows) * r[None]
                ds = p * (dprob[place, lanes].reshape(piece // 16, 16, rows) - de[None])
                prob[place, lanes] = p.reshape(piece, rows)
                dprob[place, lanes] = ds.reshape(piece, rows)
            return 0

        lax.fori_loop(0, tiles, tile, 0, unroll=True)
        place = pl.ds(slot * rows, rows)
        key_term = dot_nt(qgt[0], dprob[place, :]).T * scale
        value_term = dot_nt(qgt[1], prob[place, :]).T
        return key_term, value_term

    term_copies = []
    for slot, device in ((1, beside), (3, (down, across)), (2, (down, inner))):
        key_term, value_term = gradients(slot)
        term[slot - 1, 0] = key_term.astype(BF16)
        term[slot - 1, 1] = value_term.astype(BF16)
        c = remote(
            term.at[slot - 1],
            term_in.at[slot - 1],
            term_send.at[slot - 1],
            term_recv.at[slot - 1],
            device,
        )
        c.start()
        term_copies.append(c)
    key_term, value_term = gradients(0)
    own_term[0] = key_term
    own_term[1] = value_term

    def query_gradient(t):
        lanes = pl.ds(pl.multiple_of(t * rows, rows), rows)
        return dot_nn(kt[...], dprob[:, lanes]).T * scale

    def theirs_step(h, _):
        dq_out[:, pl.ds(pl.multiple_of(h * width, width), width)] = query_gradient(heads + h).astype(BF16)
        return 0

    lax.fori_loop(0, heads, theirs_step, 0, unroll=True)
    dq_copy = remote(dq_out, dq_in, dq_sem.at[0], dq_sem.at[1], sibling)
    dq_copy.start()
    dq_own = [query_gradient(h) for h in range(heads)]
    dq_copy.wait()
    for h in range(heads):
        lanes = pl.ds(h * width, width)
        dq_ref[:, lanes] = (dq_own[h] + dq_in[:, lanes].astype(F32)).astype(BF16)

    for c in term_copies:
        c.wait()
    dk_ref[...] = (
        own_term[0] + (term_in[0, 0].astype(F32) + term_in[1, 0].astype(F32) + term_in[2, 0].astype(F32))
    ).astype(BF16)
    dv_ref[...] = (
        own_term[1] + (term_in[0, 1].astype(F32) + term_in[1, 1].astype(F32) + term_in[2, 1].astype(F32))
    ).astype(BF16)
    for _, c in kv_sends:
        c.wait_send()
    for c in qg_all:
        c.wait_send()


def solution(mesh):
    outer_count = mesh.shape["outer"]

    def per_device(query_rows, key_rows, value_rows, out_grad, piece_ids, key_pieces):
        rows, width = key_rows.shape
        heads = query_rows.shape[1] // width
        tiles = 2 * heads
        lanes = tiles * rows
        vmem = pl.BlockSpec(memory_space=pltpu.VMEM)
        return pl.pallas_call(
            functools.partial(kernel, outer_count, heads),
            out_shape=[
                jax.ShapeDtypeStruct(query_rows.shape, BF16),
                jax.ShapeDtypeStruct(key_rows.shape, BF16),
                jax.ShapeDtypeStruct(key_rows.shape, BF16),
            ],
            in_specs=[pl.BlockSpec(memory_space=pltpu.HBM)] * 6,
            out_specs=[vmem] * 3,
            scratch_shapes=[
                pltpu.VMEM((2, 4, rows, width), BF16),
                pltpu.VMEM((2, lanes, width), BF16),
                pltpu.VMEM((2, width, lanes), BF16),
                pltpu.VMEM((width, 4 * rows), BF16),
                pltpu.VMEM((4 * rows, lanes), BF16),
                pltpu.VMEM((4 * rows, lanes), BF16),
                pltpu.VMEM((tiles, 8, 8, rows), F32),
                pltpu.VMEM((tiles, 8, 8, rows), F32),
                pltpu.VMEM((tiles, 8, 8, rows), F32),
                pltpu.VMEM((2, 8, 8, rows), F32),
                pltpu.VMEM((2, 3, tiles, rows), F32),
                pltpu.VMEM((tiles, rows), F32),
                pltpu.VMEM((16, lanes), BF16),
                pltpu.VMEM((3, 2, rows, width), BF16),
                pltpu.VMEM((3, 2, rows, width), BF16),
                pltpu.VMEM((2, rows, width), F32),
                pltpu.VMEM(query_rows.shape, BF16),
                pltpu.VMEM(query_rows.shape, BF16),
                pltpu.SMEM(piece_ids.shape, jnp.int32),
                pltpu.VMEM(key_pieces.shape, jnp.int32),
                pltpu.SemaphoreType.DMA((6,)),
                pltpu.SemaphoreType.DMA((8,)),
                pltpu.SemaphoreType.DMA((8,)),
                pltpu.SemaphoreType.DMA((2,)),
                pltpu.SemaphoreType.DMA((2,)),
                pltpu.SemaphoreType.DMA((2,)),
                pltpu.SemaphoreType.DMA((3,)),
                pltpu.SemaphoreType.DMA((3,)),
                pltpu.SemaphoreType.DMA((2,)),
            ],
            compiler_params=pltpu.CompilerParams(
                collective_id=0, has_side_effects=True, vmem_limit_bytes=64 * 1024 * 1024
            ),
            name="attention_backward",
        )(query_rows, out_grad, key_rows, value_rows, piece_ids, key_pieces)

    return jax.shard_map(
        per_device,
        mesh=mesh,
        in_specs=(
            P(("outer", "inner"), None),
            P(("outer", "inner"), None),
            P(("outer", "inner"), None),
            P(("outer", "inner"), None),
            P(),
            P("outer", None),
        ),
        out_specs=(
            P(("outer", "inner"), None),
            P(("outer", "inner"), None),
            P(("outer", "inner"), None),
        ),
        check_vma=False,
    )
```

time: 186 us -> 38.5 us (0.21); the launches traced: 184 us -> 38.3 us
  matrix products: 73.3 us -> 0 us
  waiting for transfers between devices: 63.2 us -> 0 us
  Pallas kernels: 0 us -> 34.3 us
  between operations: 14.2 us -> 0.65 us
  other arithmetic: 13.3 us -> 0 us
  starting transfers between devices: 10 us -> 0 us
  local copies, waits for them, and re-layouts: 8.87 us -> 3.4 us
    dot_general x56 -> x0, matrix products: 73.3 us -> none  [the longest x8 23.8 us: output_step(): jnp.einsum('hqk,kd->qhd', weights_low, value_set, preferred_element_type=...]
    pallas_call x0 -> x1, Pallas kernels: none -> 34.3 us  [per_device(): pl.pallas_call(functools.partial(kernel, outer_count, heads), out_shape=[...]
    reduce_scatter x1 -> x0, waiting for transfers between devices: 31.8 us -> none  [per_device(): lax.psum_scatter(kv_terms, 'inner', scatter_dimension=0, tiled=True)]
    ppermute x2 -> x0, waiting for transfers between devices: 16.2 us -> none  [shifted(): return lax.ppermute(x, axis, [(i, (i + by) % count) for i in range(count)])]
    all_gather x1 -> x0, waiting for transfers between devices: 15.1 us -> none  [per_device(): lax.all_gather(both_sets[None], 'inner', axis=0, tiled=True)]
    ppermute x2 -> x0, starting transfers between devices: 9.94 us -> none  [shifted(): return lax.ppermute(x, axis, [(i, (i + by) % count) for i in range(count)])]
    dynamic_update_slice x8 -> x0, other arithmetic: 5.8 us -> none  [per_device(): lax.scan(back_step, jnp.zeros((row_count, head_count, head_width), jnp.fl...]
    reduce_sum x9 -> x0, other arithmetic: 4.91 us -> none  [the longest x8 3.54 us: stat_step(): jnp.sum(jnp.where(allowed[None], jnp.exp(scores - running_max[:, :, None]...]
  transfers between devices with their start and end apart: 4 -> 0, of which waited for: 4 -> 0; matrix products, arithmetic and copies ran while one was open for 3% -> 0% of each run, Pallas kernels for 0% -> 0%
where the time goes in v1:
time: 38.5 us; the launch traced here: 38.3 us
  Pallas kernels  34.3 us (89%)
  local copies, waits for them, and re-layouts  3.4 us (9%)
  between operations  0.65 us (2%)
    pallas_call x1, Pallas kernels, per_device(): pl.pallas_call(functools.partial(kernel, outer_count, heads), out_shape=[...  34.3 us
    unnamed x7, local copies, waits for them, and re-layouts  3.4 us

profile of v1, /device:TPU:1, one launch (start us, length us, event | category | flops | bytes accessed | tf_op | source)
XLA Modules:
  0.0 38.3 jit_solution(17900935089743287866)
XLA Ops:
  0.6 34.3 %attention_backward.1 = (bf16[256,1024]{1,0:T(8,128)(2,1)}, bf16[256,128]{1,0:T(8,128)(2,1)}, bf16[256,128]{1,0:T(8,128)(2,1)}) custom-call(bf16[256,1024]{1,0:T(8,128)(2,1)} %q_ref.1, bf16[256,1024]{1,0:T(8,128)(2,1)} %g_ref.1, bf16[256,128]{1,0:T(8,128)(2,1)} %k_ref.1, bf16[256,128]{1,0:T(8,128)(2,1)} %v_ref.1, s32[512]{0:T(512)} %ids_hbm.1, s32[8,16]{1,0:T(8,128)} %lists_hbm.1), custom_call_target="tpu_custom_call" | custom-call | tf_op jit(solution)/shard_map/attention_backward/pallas_call | solution.py:339
  34.9 0.0 copy-start.1
  34.9 1.9 %copy.12 = bf16[256,1024]{1,0:T(8,128)(2,1)} copy(bf16[256,1024]{1,0:T(8,128)(2,1)} %get-tuple-element.6) | data formatting | bytes 1048576
  36.8 0.0 copy-done.1
  36.8 0.0 copy-start
  36.8 0.6 %copy.13 = bf16[256,128]{1,0:T(8,128)(2,1)} copy(bf16[256,128]{1,0:T(8,128)(2,1)S(1)} %copy-done.1) | data formatting | bytes 131072
  37.4 0.2 copy-done
  37.7 0.6 %copy.14 = bf16[256,128]{1,0:T(8,128)(2,1)} copy(bf16[256,128]{1,0:T(8,128)(2,1)S(1)} %copy-done) | data formatting | bytes 131072
Async XLA Ops:
  34.9 1.9 %copy-start.1 = (bf16[256,128]{1,0:T(8,128)(2,1)S(1)}, bf16[256,128]{1,0:T(8,128)(2,1)}, u32[]{:S(2)}) copy-start(bf16[256,128]{1,0:T(8,128)(2,1)} %get-tuple-element.7) | copy-start | bytes 196612
  36.8 0.9 %copy-start = (bf16[256,128]{1,0:T(8,128)(2,1)S(1)}, bf16[256,128]{1,0:T(8,128)(2,1)}, u32[]{:S(2)}) copy-start(bf16[256,128]{1,0:T(8,128)(2,1)} %get-tuple-element.8) | copy-start | bytes 196612

commit v2 on v1

--- a/solution.py
+++ b/solution.py
@@ -36,7 +36,6 @@
     dv_ref,
     kv,
     qg,
-    qgt,
     kt,
     prob,
     dprob,
@@ -45,11 +44,11 @@
     dtotal,
     bias,
     stat,
+    dstat,
     factor,
     delta,
     term,
     term_in,
-    own_term,
     dq_out,
     dq_in,
     ids_ref,
@@ -60,9 +59,11 @@
     qg_send,
     qg_recv,
     stat_sem,
+    dstat_sem,
     term_send,
     term_recv,
-    dq_sem,
+    dq_send,
+    dq_recv,
 ):
     rows = k_ref.shape[0]
     width = k_ref.shape[1]
@@ -113,18 +114,21 @@
         c.start()
 
     barrier = pltpu.get_barrier_semaphore()
-    for device in (sibling, beside, (up, inner), (down, inner), (up, across), (down, across)):
+    for device in (sibling, beside, (down, inner), (down, across)):
         pl.semaphore_signal(barrier, inc=1, device_id=device, device_id_type=MESH)
-    pl.semaphore_wait(barrier, 6)
-
-    kv_sends = []
-    for slot, device in ((2, (up, inner)), (3, (up, across)), (1, beside)):
-        for which, src in ((0, k_ref), (1, v_ref)):
+    pl.semaphore_wait(barrier, 4)
+
+    for c in loads_kv:
+        c.wait()
+    kv_copies = {}
+    for which in range(2):
+        for slot, device in ((2, (up, inner)), (3, (up, across)), (1, beside)):
             index = 2 * slot + which
-            c = remote(src, kv.at[which, slot], kv_send.at[index], kv_recv.at[index], device)
-            c.start()
-            kv_sends.append((index, c))
-    by_index = dict(kv_sends)
+            kv_copies[slot, which] = remote(
+                kv.at[which, 0], kv.at[which, slot], kv_send.at[index], kv_recv.at[index], device
+            )
+    for slot in (2, 3, 1):
+        kv_copies[slot, 0].start()
     for which, src in ((0, q_ref), (1, g_ref)):
         for h in range(heads):
             c = remote(
@@ -164,34 +168,34 @@
             t = who * heads + h
             lanes = pl.ds(pl.multiple_of(t * rows, rows), rows)
             s = dot_nt(kv[0, slot], qg[0, lanes, :])
-            g = dot_nt(kv[1, slot], qg[1, lanes, :])
             for a in range(2):
                 sa = s[a * piece : (a + 1) * piece]
-                ga = g[a * piece : (a + 1) * piece]
                 if slot == 0 and who == 0:
                     cut = jnp.where(causal, sa[:, a * piece : (a + 1) * piece], FILL)
                     sa = jnp.concatenate(
                         [cut, sa[:, piece:]] if a == 0 else [sa[:, :piece], cut], axis=1
                     )
                 s3 = sa.reshape(piece // 8, 8, rows)
-                g3 = ga.reshape(piece // 8, 8, rows)
                 m = jnp.max(s3, axis=0)
                 p = jnp.exp2((s3 - m[None]) * scale2)
-                place = pl.ds(slot * rows + a * piece, piece)
-                prob[place, lanes] = p.reshape(piece, rows).astype(BF16)
-                dprob[place, lanes] = ga.astype(BF16)
+                prob[pl.ds(slot * rows + a * piece, piece), lanes] = p.reshape(piece, rows).astype(BF16)
                 top[t, 2 * slot + a] = m * scale2
                 total[t, 2 * slot + a] = jnp.sum(p, axis=0)
-                dtotal[t, 2 * slot + a] = jnp.sum(p * g3, axis=0)
             return 0
 
         lax.fori_loop(0, heads, head, 0, unroll=True)
 
-    def transposed(who):
+    def dscores_part(slot, who):
         def head(h, _):
-            lanes = pl.ds(pl.multiple_of((who * heads + h) * rows, rows), rows)
-            qgt[0, :, lanes] = qg[0, lanes, :].T
-            qgt[1, :, lanes] = qg[1, lanes, :].T
+            t = who * heads + h
+            lanes = pl.ds(pl.multiple_of(t * rows, rows), rows)
+            g = dot_nt(kv[1, slot], qg[1, lanes, :])
+            for a in range(2):
+                ga = g[a * piece : (a + 1) * piece]
+                place = pl.ds(slot * rows + a * piece, piece)
+                p = prob[place, lanes].astype(F32).reshape(piece // 8, 8, rows)
+                dprob[place, lanes] = ga.astype(BF16)
+                dtotal[t, 2 * slot + a] = jnp.sum(p * ga.reshape(piece // 8, 8, rows), axis=0)
             return 0
 
         lax.fori_loop(0, heads, head, 0, unroll=True)
@@ -199,15 +203,11 @@
     def transposed_keys(slot):
         kt[:, pl.ds(slot * rows, rows)] = kv[0, slot].T
 
-    for c in loads_kv:
-        c.wait()
-    for which in range(2):
+    def loaded(which):
         pltpu.make_async_copy(
             qg.at[which, pl.ds(half, half)], qg.at[which, pl.ds(0, half)], load_sem.at[2 + which]
         ).wait()
-    scores(0, 0)
-    transposed(0)
-    transposed_keys(0)
+
     qg_all = [
         remote(
             qg.at[which, pl.ds(0, half)],
@@ -218,16 +218,29 @@
         )
         for which in range(2)
     ]
-    for c in qg_all:
-        c.wait_recv()
+
+    transposed_keys(0)
+    loaded(0)
+    scores(0, 0)
+    qg_all[0].wait_recv()
     scores(0, 1)
-    transposed(1)
-    for slot in (1, 2, 3):
-        for which in range(2):
-            by_index[2 * slot + which].wait_recv()
-        scores(slot, 0)
-        scores(slot, 1)
-        transposed_keys(slot)
+    for slot in (2, 3, 1):
+        kv_copies[slot, 1].start()
+    loaded(1)
+    dscores_part(0, 0)
+    qg_all[1].wait_recv()
+    dscores_part(0, 1)
+    kv_copies[1, 0].wait_recv()
+    scores(1, 0)
+    scores(1, 1)
+    transposed_keys(1)
+    kv_copies[2, 0].wait_recv()
+    scores(2, 0)
+    scores(2, 1)
+    transposed_keys(2)
+    kv_copies[3, 0].wait_recv()
+    scores(3, 0)
+    scores(3, 1)
 
     for who in range(2):
 
@@ -239,89 +252,134 @@
             top[t] = w
             stat[0, 0, pl.ds(t, 1)] = m
             stat[0, 1, pl.ds(t, 1)] = jnp.sum(jnp.sum(w * total[t], axis=0), axis=0, keepdims=True)
-            stat[0, 2, pl.ds(t, 1)] = jnp.sum(jnp.sum(w * dtotal[t], axis=0), axis=0, keepdims=True)
             return 0
 
         lax.fori_loop(0, heads, local, 0, unroll=True)
     stat_copy = remote(stat.at[0], stat.at[1], stat_sem.at[0], stat_sem.at[1], sibling)
     stat_copy.start()
+
+    transposed_keys(3)
+    kv_copies[1, 1].wait_recv()
+    dscores_part(1, 0)
+    dscores_part(1, 1)
+    kv_copies[2, 1].wait_recv()
+    dscores_part(2, 0)
+    dscores_part(2, 1)
+
+    def swapped(x):
+        return jnp.concatenate([x[heads:], x[:heads]], axis=0)
+
     stat_copy.wait()
-    mine = [stat[0, c] for c in range(3)]
-    theirs = [jnp.concatenate([stat[1, c, heads:], stat[1, c, :heads]], axis=0) for c in range(3)]
-    m = jnp.maximum(mine[0], theirs[0])
-    e_mine = jnp.exp2(mine[0] - m)
-    e_theirs = jnp.exp2(theirs[0] - m)
-    inverse = 1.0 / (mine[1] * e_mine + theirs[1] * e_theirs)
-    factor[...] = e_mine * inverse
-    d = (mine[2] * e_mine + theirs[2] * e_theirs) * inverse
-    for t in range(tiles):
-        delta[:, pl.ds(t * rows, rows)] = jnp.broadcast_to(d[t : t + 1], (16, rows)).astype(BF16)
-
-    def gradients(slot):
-        def tile(t, _):
+    m_mine, m_theirs = stat[0, 0], swapped(stat[1, 0])
+    m = jnp.maximum(m_mine, m_theirs)
+    e_mine = jnp.exp2(m_mine - m)
+    norm = stat[0, 1] * e_mine + swapped(stat[1, 1]) * jnp.exp2(m_theirs - m)
+    factor[...] = e_mine * (1.0 / norm)
+
+    term_copies = {}
+    for slot, device in ((1, beside), (3, (down, across)), (2, (down, inner))):
+        for which in range(2):
+            index = 2 * (slot - 1) + which
+            term_copies[slot, which] = remote(
+                term.at[slot - 1, which],
+                term_in.at[slot - 1, which],
+                term_send.at[index],
+                term_recv.at[index],
+                device,
+            )
+
+    def value_gradient(slot):
+        def tile(t, value_term):
             lanes = pl.ds(pl.multiple_of(t * rows, rows), rows)
             f = factor[pl.ds(t, 1)]
-            de = delta[:, lanes]
+            weights = []
             for a in range(2):
                 r = (top[t, 2 * slot + a] * f).astype(BF16)
                 r = jnp.concatenate([r, r], axis=0)
                 place = pl.ds(slot * rows + a * piece, piece)
                 p = prob[place, lanes].reshape(piece // 16, 16, rows) * r[None]
-                ds = p * (dprob[place, lanes].reshape(piece // 16, 16, rows) - de[None])
-                prob[place, lanes] = p.reshape(piece, rows)
-                dprob[place, lanes] = ds.reshape(piece, rows)
-            return 0
-
-        lax.fori_loop(0, tiles, tile, 0, unroll=True)
-        place = pl.ds(slot * rows, rows)
-        key_term = dot_nt(qgt[0], dprob[place, :]).T * scale
-        value_term = dot_nt(qgt[1], prob[place, :]).T
-        return key_term, value_term
-
-    term_copies = []
-    for slot, device in ((1, beside), (3, (down, across)), (2, (down, inner))):
-        key_term, value_term = gradients(slot)
-        term[slot - 1, 0] = key_term.astype(BF16)
+                weights.append(p.reshape(piece, rows))
+            p = jnp.concatenate(weights, axis=0)
+            prob[pl.ds(slot * rows, rows), lanes] = p
+            return value_term + dot_nn(p, qg[1, lanes, :])
+
+        value_term = lax.fori_loop(0, tiles, tile, jnp.zeros((rows, width), F32), unroll=True)
+        if slot == 0:
+            return value_term
         term[slot - 1, 1] = value_term.astype(BF16)
-        c = remote(
-            term.at[slot - 1],
-            term_in.at[slot - 1],
-            term_send.at[slot - 1],
-            term_recv.at[slot - 1],
-            device,
-        )
-        c.start()
-        term_copies.append(c)
-    key_term, value_term = gradients(0)
-    own_term[0] = key_term
-    own_term[1] = value_term
+        term_copies[slot, 1].start()
+
+    value_gradient(1)
+    kv_copies[3, 1].wait_recv()
+    dscores_part(3, 0)
+    dscores_part(3, 1)
+
+    def dlocal(t, _):
+        d = jnp.sum(jnp.sum(top[t] * dtotal[t], axis=0), axis=0, keepdims=True)
+        dstat[0, pl.ds(t, 1)] = d * factor[pl.ds(t, 1)]
+        return 0
+
+    lax.fori_loop(0, tiles, dlocal, 0, unroll=True)
+    dstat_copy = remote(dstat.at[0], dstat.at[1], dstat_sem.at[0], dstat_sem.at[1], sibling)
+    dstat_copy.start()
+    value_gradient(2)
+    value_gradient(3)
+    own_value = value_gradient(0)
+    dstat_copy.wait()
+    d = dstat[0] + swapped(dstat[1])
+    for t in range(tiles):
+        delta[:, pl.ds(t * rows, rows)] = jnp.broadcast_to(d[t : t + 1], (16, rows)).astype(BF16)
+
+    def key_gradient(slot, who, key_term):
+        def tile(h, key_term):
+            t = who * heads + h
+            lanes = pl.ds(pl.multiple_of(t * rows, rows), rows)
+            place = pl.ds(slot * rows, rows)
+            de = delta[:, lanes]
+            ds = prob[place, lanes].reshape(rows // 16, 16, rows) * (
+                dprob[place, lanes].reshape(rows // 16, 16, rows) - de[None]
+            )
+            ds = ds.reshape(rows, rows)
+            dprob[place, lanes] = ds
+            return key_term + dot_nn(ds, qg[0, lanes, :])
+
+        return lax.fori_loop(0, heads, tile, key_term, unroll=True)
+
+    def key_send(slot, key_term):
+        term[slot - 1, 0] = (key_term * scale).astype(BF16)
+        term_copies[slot, 0].start()
 
     def query_gradient(t):
         lanes = pl.ds(pl.multiple_of(t * rows, rows), rows)
         return dot_nn(kt[...], dprob[:, lanes]).T * scale
 
-    def theirs_step(h, _):
-        dq_out[:, pl.ds(pl.multiple_of(h * width, width), width)] = query_gradient(heads + h).astype(BF16)
-        return 0
-
-    lax.fori_loop(0, heads, theirs_step, 0, unroll=True)
-    dq_copy = remote(dq_out, dq_in, dq_sem.at[0], dq_sem.at[1], sibling)
-    dq_copy.start()
+    zero = jnp.zeros((rows, width), F32)
+    key_send(1, key_gradient(1, 0, key_gradient(1, 1, zero)))
+    partial = {slot: key_gradient(slot, 1, zero) for slot in (2, 3, 0)}
+    dq_copies = []
+    for c in range(4):
+        for h in (2 * c, 2 * c + 1):
+            dq_out[:, h * width : (h + 1) * width] = query_gradient(heads + h).astype(BF16)
+        lanes = pl.ds(2 * c * width, 2 * width)
+        copy = remote(dq_out.at[:, lanes], dq_in.at[:, lanes], dq_send.at[c], dq_recv.at[c], sibling)
+        copy.start()
+        dq_copies.append(copy)
+    for slot in (2, 3):
+        key_send(slot, key_gradient(slot, 0, partial[slot]))
+    own_key = key_gradient(0, 0, partial[0]) * scale
     dq_own = [query_gradient(h) for h in range(heads)]
-    dq_copy.wait()
-    for h in range(heads):
-        lanes = pl.ds(h * width, width)
-        dq_ref[:, lanes] = (dq_own[h] + dq_in[:, lanes].astype(F32)).astype(BF16)
-
-    for c in term_copies:
+    for c in range(4):
+        dq_copies[c].wait()
+        for h in (2 * c, 2 * c + 1):
+            lanes = pl.ds(h * width, width)
+            dq_ref[:, lanes] = (dq_own[h] + dq_in[:, lanes].astype(F32)).astype(BF16)
+
+    for c in term_copies.values():
         c.wait()
-    dk_ref[...] = (
-        own_term[0] + (term_in[0, 0].astype(F32) + term_in[1, 0].astype(F32) + term_in[2, 0].astype(F32))
-    ).astype(BF16)
-    dv_ref[...] = (
-        own_term[1] + (term_in[0, 1].astype(F32) + term_in[1, 1].astype(F32) + term_in[2, 1].astype(F32))
-    ).astype(BF16)
-    for _, c in kv_sends:
+    for which, own, out in ((0, own_key, dk_ref), (1, own_value, dv_ref)):
+        others = term_in[0, which].astype(F32) + term_in[1, which].astype(F32)
+        out[...] = (own + (others + term_in[2, which].astype(F32))).astype(BF16)
+    for c in kv_copies.values():
         c.wait_send()
     for c in qg_all:
         c.wait_send()
@@ -348,7 +406,6 @@
             scratch_shapes=[
                 pltpu.VMEM((2, 4, rows, width), BF16),
                 pltpu.VMEM((2, lanes, width), BF16),
-                pltpu.VMEM((2, width, lanes), BF16),
                 pltpu.VMEM((width, 4 * rows), BF16),
                 pltpu.VMEM((4 * rows, lanes), BF16),
                 pltpu.VMEM((4 * rows, lanes), BF16),
@@ -356,12 +413,12 @@
                 pltpu.VMEM((tiles, 8, 8, rows), F32),
                 pltpu.VMEM((tiles, 8, 8, rows), F32),
                 pltpu.VMEM((2, 8, 8, rows), F32),
-                pltpu.VMEM((2, 3, tiles, rows), F32),
+                pltpu.VMEM((2, 2, tiles, rows), F32),
+                pltpu.VMEM((2, tiles, rows), F32),
                 pltpu.VMEM((tiles, rows), F32),
                 pltpu.VMEM((16, lanes), BF16),
                 pltpu.VMEM((3, 2, rows, width), BF16),
                 pltpu.VMEM((3, 2, rows, width), BF16),
-                pltpu.VMEM((2, rows, width), F32),
                 pltpu.VMEM(query_rows.shape, BF16),
                 pltpu.VMEM(query_rows.shape, BF16),
                 pltpu.SMEM(piece_ids.shape, jnp.int32),
@@ -372,9 +429,11 @@
                 pltpu.SemaphoreType.DMA((2,)),
                 pltpu.SemaphoreType.DMA((2,)),
                 pltpu.SemaphoreType.DMA((2,)),
-                pltpu.SemaphoreType.DMA((3,)),
-                pltpu.SemaphoreType.DMA((3,)),
                 pltpu.SemaphoreType.DMA((2,)),
+                pltpu.SemaphoreType.DMA((6,)),
+                pltpu.SemaphoreType.DMA((6,)),
+                pltpu.SemaphoreType.DMA((4,)),
+                pltpu.SemaphoreType.DMA((4,)),
             ],
             compiler_params=pltpu.CompilerParams(
                 collective_id=0, has_side_effects=True, vmem_limit_bytes=64 * 1024 * 1024

time: 38.5 us -> 34.4 us (0.89)
  Pallas kernels: 34.3 us -> 30.2 us
    pallas_call x1, Pallas kernels: 34.3 us -> 30.2 us  [per_device(): pl.pallas_call(functools.partial(kernel, outer_count, heads), out_shape=[...]
where the time goes in v2:
time: 34.4 us; the launch traced here: 34.2 us
  Pallas kernels  30.2 us (88%)
  local copies, waits for them, and re-layouts  3.4 us (10%)
  between operations  0.65 us (2%)
    pallas_call x1, Pallas kernels, per_device(): pl.pallas_call(functools.partial(kernel, outer_count, heads), out_shape=[...  30.2 us
    unnamed x7, local copies, waits for them, and re-layouts  3.4 us

profile of v2, /device:TPU:1, one launch (start us, length us, event | category | flops | bytes accessed | tf_op | source)
XLA Modules:
  0.0 34.2 jit_solution(16302473042268150100)
XLA Ops:
  0.6 30.2 %attention_backward.1 = (bf16[256,1024]{1,0:T(8,128)(2,1)}, bf16[256,128]{1,0:T(8,128)(2,1)}, bf16[256,128]{1,0:T(8,128)(2,1)}) custom-call(bf16[256,1024]{1,0:T(8,128)(2,1)} %q_ref.1, bf16[256,1024]{1,0:T(8,128)(2,1)} %g_ref.1, bf16[256,128]{1,0:T(8,128)(2,1)} %k_ref.1, bf16[256,128]{1,0:T(8,128)(2,1)} %v_ref.1, s32[512]{0:T(512)} %ids_hbm.1, s32[8,16]{1,0:T(8,128)} %lists_hbm.1), custom_call_target="tpu_custom_call" | custom-call | tf_op jit(solution)/shard_map/attention_backward/pallas_call | solution.py:397
  30.8 0.0 copy-start.1
  30.8 1.9 %copy.12 = bf16[256,1024]{1,0:T(8,128)(2,1)} copy(bf16[256,1024]{1,0:T(8,128)(2,1)} %get-tuple-element.6) | data formatting | bytes 1048576
  32.8 0.0 copy-done.1
  32.8 0.0 copy-start
  32.8 0.6 %copy.13 = bf16[256,128]{1,0:T(8,128)(2,1)} copy(bf16[256,128]{1,0:T(8,128)(2,1)S(1)} %copy-done.1) | data formatting | bytes 131072
  33.4 0.2 copy-done
  33.6 0.6 %copy.14 = bf16[256,128]{1,0:T(8,128)(2,1)} copy(bf16[256,128]{1,0:T(8,128)(2,1)S(1)} %copy-done) | data formatting | bytes 131072
Async XLA Ops:
  30.8 1.9 %copy-start.1 = (bf16[256,128]{1,0:T(8,128)(2,1)S(1)}, bf16[256,128]{1,0:T(8,128)(2,1)}, u32[]{:S(2)}) copy-start(bf16[256,128]{1,0:T(8,128)(2,1)} %get-tuple-element.7) | copy-start | bytes 196612
  32.8 0.9 %copy-start = (bf16[256,128]{1,0:T(8,128)(2,1)S(1)}, bf16[256,128]{1,0:T(8,128)(2,1)}, u32[]{:S(2)}) copy-start(bf16[256,128]{1,0:T(8,128)(2,1)} %get-tuple-element.8) | copy-start | bytes 196612

commit v3 on v2

--- a/solution.py
+++ b/solution.py
@@ -436,10 +436,10 @@
                 pltpu.SemaphoreType.DMA((4,)),
             ],
             compiler_params=pltpu.CompilerParams(
-                collective_id=0, has_side_effects=True, vmem_limit_bytes=64 * 1024 * 1024
+                collective_id=0, has_side_effects=True, vmem_limit_bytes=48 * 1024 * 1024
             ),
             name="attention_backward",
-        )(query_rows, out_grad, key_rows, value_rows, piece_ids, key_pieces)
+        )(*[pltpu.with_memory_space_constraint(x, pltpu.HBM) for x in (query_rows, out_grad, key_rows, value_rows, piece_ids, key_pieces)])
 
     return jax.shard_map(
         per_device,

time: 34.4 us -> 32.2 us (0.936)
  local copies, waits for them, and re-layouts: 3.4 us -> 2.05 us
  Pallas kernels: 30.2 us -> 29.4 us
    unnamed x7 -> x3, local copies, waits for them, and re-layouts: 3.4 us -> 2.05 us
    pallas_call x1, Pallas kernels: 30.2 us -> 29.4 us  [per_device(): pl.pallas_call(functools.partial(kernel, outer_count, heads), out_shape=[...]
where the time goes in v3:
time: 32.2 us; the launch traced here: 32 us
  Pallas kernels  29.4 us (91%)
  local copies, waits for them, and re-layouts  2.05 us (6%)
  between operations  0.64 us (2%)
    pallas_call x1, Pallas kernels, per_device(): pl.pallas_call(functools.partial(kernel, outer_count, heads), out_shape=[...  29.4 us
    unnamed x3, local copies, waits for them, and re-layouts  2.05 us

profile of v3, /device:TPU:1, one launch (start us, length us, event | category | flops | bytes accessed | tf_op | source)
XLA Modules:
  0.0 32.0 jit_solution(8048310002850331911)
XLA Ops:
  0.6 29.4 %attention_backward.1 = (bf16[256,1024]{1,0:T(8,128)(2,1)S(1)}, bf16[256,128]{1,0:T(8,128)(2,1)S(1)}, bf16[256,128]{1,0:T(8,128)(2,1)S(1)}) custom-call(bf16[256,1024]{1,0:T(8,128)(2,1)} %q_ref.1, bf16[256,1024]{1,0:T(8,128)(2,1)} %g_ref.1, bf16[256,128]{1,0:T(8,128)(2,1)} %k_ref.1, bf16[256,128]{1,0:T(8,128)(2,1)} %v_ref.1, s32[512]{0:T(512)} %ids_hbm.1, ...), custom_call_target="tpu_custom_call" | custom-call | tf_op jit(solution)/shard_map/attention_backward/pallas_call | solution.py:397
  30.0 0.8 %copy.12 = bf16[256,1024]{1,0:T(8,128)(2,1)} copy(bf16[256,1024]{1,0:T(8,128)(2,1)S(1)} %get-tuple-element.6) | data formatting | bytes 1048576
  30.8 0.6 %copy.13 = bf16[256,128]{1,0:T(8,128)(2,1)} copy(bf16[256,128]{1,0:T(8,128)(2,1)S(1)} %get-tuple-element.7) | data formatting | bytes 131072
  31.4 0.6 %copy.14 = bf16[256,128]{1,0:T(8,128)(2,1)} copy(bf16[256,128]{1,0:T(8,128)(2,1)S(1)} %get-tuple-element.8) | data formatting | bytes 131072
